TPU v7x, 256 devices: a whole 4x4x8 slice. The times are simulated.
256 devices in a mesh: grp: 16 (over x_hi, y, core), dev: 16 (over x_lo, z).
Axes of the slice: x: 4 (x_hi: 2, x_lo: 2; x = x_hi * 2 + x_lo), y: 4, z: 8, core: 2. Of those that a mesh axis runs over, the one named last changes fastest.
Arguments:
- series: bfloat16 [16384, 6, 1024], P(('grp', 'dev')), may hold values from -6 to 6
- taps: bfloat16 [16384, 64], P(('grp', 'dev')), may hold values from -0.75 to 0.75
- keep: int32 [16384, 6], P(('grp', 'dev')), may hold values from 0 to 1, as said below
- offsets: int32 [8], replicated, may hold values from 1 to 256, as said below
Outputs:
- corr: float32 [16384, 8, 128], P(('grp', 'dev'))
- stack: float32 [8, 128], replicated
Inputs may be any that keep to these rules, and one draw needn't show every extreme that they name: keep[c, s] is 1 where segment s of channel c is free of passing trains and usable; trains cover runs of neighbouring channels. 8 distinct channel offsets; 256 is always among them.
All inputs are finite; a program needn't handle non-finite values.
Results may differ from a plain program's by a relative error of at most 0.0041.
Values may be sent and summed in bfloat16 or wider, within the bound.
A program may use at most 128 MiB of HBM per device.

v0:
```python
import math
import jax
import jax.numpy as jnp
from jax import lax
from jax.sharding import PartitionSpec as P

SEG = 6
SAMP = 1024
BLK = 128
NLAG = 128
REACH = 256


def shifted(block, axis, distance):
    devices = range(lax.axis_size(axis))
    route = [((i - distance) % len(devices), i) for i in devices]
    return lax.ppermute(block, axis, route)


def toeplitz_rows(taps_part, block_len):
    row_total = taps_part.shape[0]
    tap_count = taps_part.shape[1]
    lead_zeros = jnp.zeros((row_total, block_len - tap_count + 1), taps_part.dtype)
    trail_zeros = jnp.zeros((row_total, block_len), taps_part.dtype)
    pattern = jnp.concatenate([lead_zeros, taps_part[:, ::-1], trail_zeros], axis=1)
    repeated = jnp.tile(pattern, (1, block_len))
    return repeated[:, : block_len * 2 * block_len].reshape(row_total, block_len, 2 * block_len)


def whiten_local(series_part, taps_part):
    row_total, segment_count, sample_count = series_part.shape
    blocks = series_part.reshape(row_total, segment_count, sample_count // BLK, BLK)
    earlier = jnp.concatenate([jnp.zeros_like(blocks[:, :, :1]), blocks[:, :, :-1]], axis=2)
    windows = jnp.concatenate([earlier, blocks], axis=3)
    matrix = toeplitz_rows(taps_part, BLK)
    filtered = jnp.einsum("csbi,cji->csbj", windows, matrix, preferred_element_type=jnp.float32)
    return filtered.reshape(row_total, segment_count, sample_count).astype(jnp.bfloat16)


def forward_table(input_len):
    transform_size = 2 * BLK
    sample_index = jnp.arange(input_len, dtype=jnp.int32)[:, None]
    cos_bins = jnp.arange(BLK + 1, dtype=jnp.int32)[None, :]
    sin_bins = jnp.arange(1, BLK, dtype=jnp.int32)[None, :]
    cos_phase = (sample_index * cos_bins % transform_size).astype(jnp.float32) * (
        2.0 * math.pi / transform_size
    )
    sin_phase = (sample_index * sin_bins % transform_size).astype(jnp.float32) * (
        2.0 * math.pi / transform_size
    )
    return jnp.concatenate([jnp.cos(cos_phase), -jnp.sin(sin_phase)], axis=1)


def split_table(table):
    high_part = lax.optimization_barrier(table.astype(jnp.bfloat16))
    low_part = (table - high_part.astype(jnp.float32)).astype(jnp.bfloat16)
    return (high_part, low_part)


def table_product(records, parts):
    return jnp.dot(records, parts[0], preferred_element_type=jnp.float32) + jnp.dot(
        records, parts[1], preferred_element_type=jnp.float32
    )


def lag_table():
    transform_size = 2 * BLK
    lag_index = jnp.arange(NLAG, dtype=jnp.int32)[None, :]
    cos_bins = jnp.arange(BLK + 1, dtype=jnp.int32)[:, None]
    sin_bins = jnp.arange(1, BLK, dtype=jnp.int32)[:, None]
    cos_weight = jnp.where((cos_bins == 0) | (cos_bins == BLK), 1.0, 2.0) / transform_size
    cos_phase = (cos_bins * lag_index % transform_size).astype(jnp.float32) * (
        2.0 * math.pi / transform_size
    )
    sin_phase = (sin_bins * lag_index % transform_size).astype(jnp.float32) * (
        2.0 * math.pi / transform_size
    )
    cos_part = jnp.cos(cos_phase) * cos_weight
    sin_part = jnp.sin(sin_phase) * (-2.0 / transform_size)
    return jnp.concatenate([cos_part, sin_part], axis=0)


def record_spectra(records, upper_parts, lower_parts):
    row_total = records.shape[0]
    half_lag = NLAG // 2
    padded = jnp.concatenate(
        [
            jnp.zeros((row_total, half_lag), jnp.bfloat16),
            records,
            jnp.zeros((row_total, BLK - half_lag), jnp.bfloat16),
        ],
        axis=1,
    )
    pieces = padded.reshape(row_total, SAMP // BLK + 1, BLK)
    first_half = table_product(pieces[:, :-1], upper_parts)
    return first_half + table_product(pieces[:, 1:], lower_parts)


def cross_spectra(own_spectra, partner_spectra):
    edge_bins = BLK + 1
    own_real = own_spectra[..., :edge_bins]
    own_imag = own_spectra[..., edge_bins:]
    far_real = partner_spectra[..., :edge_bins]
    far_imag = partner_spectra[..., edge_bins:]
    zero_column = jnp.zeros_like(own_imag[..., :1])
    own_imag_full = jnp.concatenate([zero_column, own_imag, zero_column], axis=-1)
    far_imag_full = jnp.concatenate([zero_column, far_imag, zero_column], axis=-1)
    real_part = jnp.sum(own_real * far_real + own_imag_full * far_imag_full, axis=-2)
    imag_part = jnp.sum(own_real[..., 1:BLK] * far_imag - own_imag * far_real[..., 1:BLK], axis=-2)
    return jnp.concatenate([real_part, imag_part], axis=-1)


def local(series, taps, keep, offsets):
    channels = series.shape[0]
    hop_count = REACH // channels
    offset_total = offsets.shape[0]
    keep_wire = keep.astype(jnp.bfloat16)
    own_white = whiten_local(series, taps)
    arrived = []
    for distance in range(1, hop_count + 1):
        arrived.append(shifted((own_white, keep_wire), ("grp", "dev"), -distance))
    partner_white = [received[0] for received in arrived]
    partner_keep = [received[1] for received in arrived]
    keep_own = keep.astype(jnp.float32)
    keep_near = jnp.concatenate([keep_wire] + partner_keep, axis=0).astype(jnp.float32)
    partner_rows = offsets[:, None] + jnp.arange(channels, dtype=jnp.int32)[None, :]
    paired = keep_own[None, :, :] * keep_near[partner_rows]
    pair_count = jnp.sum(paired, axis=2)
    block_parts = split_table(forward_table(BLK))
    window_table = forward_table(2 * BLK)
    upper_parts = split_table(window_table[:BLK])
    lower_parts = split_table(window_table[BLK:])
    accumulated = jnp.zeros((offset_total, channels, 2 * BLK), jnp.float32)
    for segment in range(SEG):
        weights = paired[:, :, segment]
        nearby = jnp.concatenate(
            [own_white[:, segment]] + [white[:, segment] for white in partner_white], axis=0
        )
        near_spectra = record_spectra(nearby, upper_parts, lower_parts)
        own_blocks = own_white[:, segment].reshape(channels, SAMP // BLK, BLK)
        own_spectra = table_product(own_blocks, block_parts)

        def offset_terms(offset_value):
            partner = lax.dynamic_slice_in_dim(near_spectra, offset_value, channels, 0)
            return cross_spectra(own_spectra, partner)

        spectra_terms = lax.map(offset_terms, offsets)
        accumulated = accumulated + weights[:, :, None] * spectra_terms
    lag_values = jnp.dot(accumulated, lag_table(), precision=lax.Precision.HIGHEST)
    divisor = jnp.maximum(pair_count, 1.0)[:, :, None] * math.sqrt(SAMP)
    corr = jnp.transpose(lag_values / divisor, (1, 0, 2))
    partial_sum = jnp.sum(corr, axis=0)
    stack = lax.psum(partial_sum, ("grp", "dev")) / math.sqrt(
        channels * lax.axis_size(("grp", "dev"))
    )
    return (corr, stack)


def solution(mesh):
    in_specs = (
        P(("grp", "dev"), None, None),
        P(("grp", "dev"), None),
        P(("grp", "dev"), None),
        P(),
    )
    out_specs = (P(("grp", "dev"), None, None), P())
    return jax.shard_map(local, mesh=mesh, in_specs=in_specs, out_specs=out_specs, check_vma=False)
```

profile of v0, /device:TPU:1, one launch (start us, length us, event | category | flops | bytes accessed | tf_op | source)
XLA Modules:
  0.0 685.6 jit_solution(6252859585116331420)
XLA Ops:
  1.4 7.9 %collective-permute-start = (bf16[64,6]{0,1:T(8,128)(2,1)S(1)}, bf16[64,6]{0,1:T(8,128)(2,1)S(1)}, u32[]{:S(2)}, u32[]{:S(2)}) collective-permute-start(bf16[64,6]{0,1:T(8,128)(2,1)S(1)} %get-tuple-element.315), channel_id=1, source_target_pairs={{1,0},{2,1},{3,2},{4,3},{5,4},{6,5},{7,6},{8,7},{9,8},{10,9},{11,1... | collective-permute-start | bytes 2312 | tf_op jit(solution)/shard_map/ppermute | solution.py:17
  11.2 5.0 collective-permute-start.3
  18.0 3.2 tile.4
  21.2 10.9 %tile.10 = bf16[64,32896]{1,0:T(8,128)(2,1)} reshape(bf16[64,128,257]{2,1,0:T(8,128)(2,1)} %tile.4) | data formatting | bytes 8421376 | tf_op jit(solution)/shard_map/tile | solution.py:26
  32.0 2.2 slice-done
  54.0 9.1 %collective-permute-start.7 = (bf16[64,6,1024]{2,0,1:T(8,128)(2,1)}, bf16[64,6,1024]{2,0,1:T(8,128)(2,1)}, u32[]{:S(2)}, u32[]{:S(2)}) collective-permute-start(bf16[64,6,1024]{2,0,1:T(8,128)(2,1)} %convert_element_type.64), channel_id=1, source_target_pairs={{4,0},{5,1},{6,2},{7,3},{8,4},{9,5},{10,6},{11,7},{12,8},{13,9},{1... | collective-permute-start | bytes 2359304 | tf_op jit(solution)/shard_map/ppermute | solution.py:17
  68.3 21.4 %collective-permute-done.5 = bf16[64,6,1024]{2,0,1:T(8,128)(2,1)} collective-permute-done((bf16[64,6,1024]{2,0,1:T(8,128)(2,1)}, bf16[64,6,1024]{2,0,1:T(8,128)(2,1)}, u32[]{:S(2)}, u32[]{:S(2)}) %collective-permute-start.5) | collective-permute-done | bytes 786464 | tf_op jit(solution)/shard_map/ppermute | solution.py:17
  91.8 39.8 %collective-permute-done.6 = bf16[64,6,1024]{2,0,1:T(8,128)(2,1)} collective-permute-done((bf16[64,6,1024]{2,0,1:T(8,128)(2,1)}, bf16[64,6,1024]{2,0,1:T(8,128)(2,1)}, u32[]{:S(2)}, u32[]{:S(2)}) %collective-permute-start.6) | collective-permute-done | bytes 786464 | tf_op jit(solution)/shard_map/ppermute | solution.py:17
  135.8 2.4 concatenate.117
  140.3 2.7 fusion.189
  143.1 2.4 copy.56
  145.5 3.1 fusion.161
  150.6 2.4 concatenate.120
  155.2 2.8 fusion.190
  157.9 2.4 copy.58
  160.3 3.2 fusion.198
  165.5 2.4 concatenate.122
  170.0 2.8 fusion.191
  172.8 2.4 copy.60
  175.3 3.1 fusion.199
  180.3 2.4 concatenate.124
  184.9 2.8 fusion.192
  187.6 2.4 copy.62
  190.1 3.2 fusion.200
  195.3 2.4 concatenate.126
  199.8 2.7 fusion.193
  202.5 2.5 copy.64
  205.0 3.1 fusion.201
  210.2 2.4 concatenate.128
  212.5 2.4 copy.51
  214.9 2.7 fusion.194
  217.6 2.4 copy.66
  220.0 3.1 fusion.202
  225.2 2.4 copy.57
  229.6 3.9 add_add_fusion.5
  234.4 48.4 %while.60 = (s32[]{:T(128)}, f32[8,64,256]{2,1,0:T(8,128)}, f32[64,8,256]{2,1,0:T(8,128)S(1)}, s32[8]{0:T(128)S(1)}, f32[320,8,256]{2,1,0:T(8,128)}, /*index=5*/...) while((s32[]{:T(128)}, f32[8,64,256]{2,1,0:T(8,128)}, f32[64,8,256]{2,1,0:T(8,128)S(1)}, ...), condition=%wide.region_3.4_spmd, body=%wide.region_0.3_spmd.sunk | while | flops 788487 | bytes 2810567 | solution.py:147
  286.2 4.0 add_add_fusion.4
  290.2 43.5 %while.61 = (s32[]{:T(128)}, f32[8,64,256]{2,1,0:T(8,128)S(1)}, f32[64,8,256]{2,1,0:T(8,128)S(1)}, s32[8]{0:T(128)S(1)}, f32[320,8,256]{2,1,0:T(8,128)}, /*index...) while((s32[]{:T(128)}, f32[8,64,256]{2,1,0:T(8,128)S(1)}, ...), condition=%wide.region_7.8_spmd, body=%wide.region_4.7_spmd.sunk | while | flops 788487 | bytes 2842827 | solution.py:147
  337.8 3.9 add_add_fusion.3
  341.7 43.5 %while.62 = (s32[]{:T(128)}, f32[8,64,256]{2,1,0:T(8,128)S(1)}, f32[64,8,256]{2,1,0:T(8,128)S(1)}, s32[8]{0:T(128)S(1)}, f32[320,8,256]{2,1,0:T(8,128)}, /*index...) while((s32[]{:T(128)}, f32[8,64,256]{2,1,0:T(8,128)S(1)}, ...), condition=%wide.region_11.12_spmd, body=%wide.region_8.11_spmd.sunk | while | flops 788487 | bytes 2842827 | solution.py:147
  389.3 3.9 add_add_fusion.2
  394.0 48.4 %while.63 = (s32[]{:T(128)}, f32[8,64,256]{2,1,0:T(8,128)}, f32[64,8,256]{2,1,0:T(8,128)S(1)}, s32[8]{0:T(128)S(1)}, f32[320,8,256]{2,1,0:T(8,128)}, /*index=5*/...) while((s32[]{:T(128)}, f32[8,64,256]{2,1,0:T(8,128)}, f32[64,8,256]{2,1,0:T(8,128)S(1)}, ...), condition=%wide.region_15.16_spmd, body=%wide.region_12.15_spmd.sunk | while | flops 788487 | bytes 2810567 | solution.py:147
  444.7 4.0 add_add_fusion.1
  449.6 48.6 %while.64 = (s32[]{:T(128)}, f32[8,64,256]{2,1,0:T(8,128)}, f32[64,8,256]{2,1,0:T(8,128)S(1)}, s32[8]{0:T(128)S(1)}, f32[320,8,256]{2,1,0:T(8,128)}, /*index=5*/...) while((s32[]{:T(128)}, f32[8,64,256]{2,1,0:T(8,128)}, f32[64,8,256]{2,1,0:T(8,128)S(1)}, ...), condition=%wide.region_19.20_spmd, body=%wide.region_16.19_spmd.sunk | while | flops 788487 | bytes 2810567 | solution.py:147
  500.4 4.0 add_add_fusion
  504.5 43.5 %while.65 = (s32[]{:T(128)}, f32[8,64,256]{2,1,0:T(8,128)S(1)}, f32[64,8,256]{2,1,0:T(8,128)S(1)}, s32[8]{0:T(128)S(1)}, f32[320,8,256]{2,1,0:T(8,128)}, /*index...) while((s32[]{:T(128)}, f32[8,64,256]{2,1,0:T(8,128)S(1)}, ...), condition=%wide.region_23.24_spmd, body=%wide.region_20.23_spmd.sunk | while | flops 788487 | bytes 2842827 | solution.py:147
  548.0 2.3 fusion.196
  551.1 133.6 %psum.7 = f32[8,128]{1,0:T(8,128)S(1)} all-reduce(f32[8,128]{1,0:T(8,128)S(1)} %get-tuple-element.316), channel_id=1, replica_groups=mesh['grp'=16,'dev'=16] {'grp','dev'}, use_global_device_ids=true, to_apply=%region_26.27 | all-reduce | flops 1024 | bytes 8192 | tf_op jit(solution)/shard_map/psum | solution.py:153
  (394 shorter events, 261.8 us)
Async XLA Ops:
  0.6 17.0 %copy-start.24 = (bf16[64,64]{1,0:T(8,128)(2,1)S(1)}, bf16[64,64]{1,0:T(8,128)(2,1)}, u32[]{:S(2)}) copy-start(bf16[64,64]{1,0:T(8,128)(2,1)} %param.17) | copy-start | bytes 24580
  1.4 51.0 %collective-permute-start = (bf16[64,6]{0,1:T(8,128)(2,1)S(1)}, bf16[64,6]{0,1:T(8,128)(2,1)S(1)}, u32[]{:S(2)}, u32[]{:S(2)}) collective-permute-start(bf16[64,6]{0,1:T(8,128)(2,1)S(1)} %get-tuple-element.315), channel_id=1, source_target_pairs={{1,0},{2,1},{3,2},{4,3},{5,4},{6,5},{7,6},{8,7},{9,8},{10,9},{11,1... | collective-permute-start | bytes 2312 | tf_op jit(solution)/shard_map/ppermute | solution.py:17
  9.3 43.8 %collective-permute-start.1 = (bf16[64,6]{0,1:T(8,128)(2,1)S(1)}, bf16[64,6]{0,1:T(8,128)(2,1)S(1)}, u32[]{:S(2)}, u32[]{:S(2)}) collective-permute-start(bf16[64,6]{0,1:T(8,128)(2,1)S(1)} %get-tuple-element.315), channel_id=1, source_target_pairs={{2,0},{3,1},{4,2},{5,3},{6,4},{7,5},{8,6},{9,7},{10,8},{11,9},{12,... | collective-permute-start | bytes 2312 | tf_op jit(solution)/shard_map/ppermute | solution.py:17
  10.8 43.3 %collective-permute-start.2 = (bf16[64,6]{0,1:T(8,128)(2,1)S(1)}, bf16[64,6]{0,1:T(8,128)(2,1)S(1)}, u32[]{:S(2)}, u32[]{:S(2)}) collective-permute-start(bf16[64,6]{0,1:T(8,128)(2,1)S(1)} %get-tuple-element.315), channel_id=1, source_target_pairs={{3,0},{4,1},{5,2},{6,3},{7,4},{8,5},{9,6},{10,7},{11,8},{12,9},{13... | collective-permute-start | bytes 2312 | tf_op jit(solution)/shard_map/ppermute | solution.py:17
  11.2 51.9 %collective-permute-start.3 = (bf16[64,6]{0,1:T(8,128)(2,1)S(1)}, bf16[64,6]{0,1:T(8,128)(2,1)S(1)}, u32[]{:S(2)}, u32[]{:S(2)}) collective-permute-start(bf16[64,6]{0,1:T(8,128)(2,1)S(1)} %get-tuple-element.315), channel_id=1, source_target_pairs={{4,0},{5,1},{6,2},{7,3},{8,4},{9,5},{10,6},{11,7},{12,8},{13,9},{1... | collective-permute-start | bytes 2312 | tf_op jit(solution)/shard_map/ppermute | solution.py:17
  32.0 2.2 slice-start
  38.3 27.8 %collective-permute-start.4 = (bf16[64,6,1024]{2,0,1:T(8,128)(2,1)}, bf16[64,6,1024]{2,0,1:T(8,128)(2,1)}, u32[]{:S(2)}, u32[]{:S(2)}) collective-permute-start(bf16[64,6,1024]{2,0,1:T(8,128)(2,1)} %convert_element_type.64), channel_id=1, source_target_pairs={{1,0},{2,1},{3,2},{4,3},{5,4},{6,5},{7,6},{8,7},{9,8},{10,9},{11,1... | collective-permute-start | bytes 2359304 | tf_op jit(solution)/shard_map/ppermute | solution.py:17
  42.9 4.6 copy-start.16
  44.8 2.0 copy-start.21
  48.4 1.2 copy-start.25
  52.4 37.2 %collective-permute-start.5 = (bf16[64,6,1024]{2,0,1:T(8,128)(2,1)}, bf16[64,6,1024]{2,0,1:T(8,128)(2,1)}, u32[]{:S(2)}, u32[]{:S(2)}) collective-permute-start(bf16[64,6,1024]{2,0,1:T(8,128)(2,1)} %convert_element_type.64), channel_id=1, source_target_pairs={{2,0},{3,1},{4,2},{5,3},{6,4},{7,5},{8,6},{9,7},{10,8},{11,9},{12,... | collective-permute-start | bytes 2359304 | tf_op jit(solution)/shard_map/ppermute | solution.py:17
  53.1 78.5 %collective-permute-start.6 = (bf16[64,6,1024]{2,0,1:T(8,128)(2,1)}, bf16[64,6,1024]{2,0,1:T(8,128)(2,1)}, u32[]{:S(2)}, u32[]{:S(2)}) collective-permute-start(bf16[64,6,1024]{2,0,1:T(8,128)(2,1)} %convert_element_type.64), channel_id=1, source_target_pairs={{3,0},{4,1},{5,2},{6,3},{7,4},{8,5},{9,6},{10,7},{11,8},{12,9},{13... | collective-permute-start | bytes 2359304 | tf_op jit(solution)/shard_map/ppermute | solution.py:17
  54.0 79.7 %collective-permute-start.7 = (bf16[64,6,1024]{2,0,1:T(8,128)(2,1)}, bf16[64,6,1024]{2,0,1:T(8,128)(2,1)}, u32[]{:S(2)}, u32[]{:S(2)}) collective-permute-start(bf16[64,6,1024]{2,0,1:T(8,128)(2,1)} %convert_element_type.64), channel_id=1, source_target_pairs={{4,0},{5,1},{6,2},{7,3},{8,4},{9,5},{10,6},{11,7},{12,8},{13,9},{1... | collective-permute-start | bytes 2359304 | tf_op jit(solution)/shard_map/ppermute | solution.py:17
  143.1 5.5 copy-start.13
  145.5 3.1 copy-start.7
  160.3 3.2 copy-start.8
  175.3 3.1 copy-start.9
  190.1 3.2 copy-start.10
  205.0 3.1 copy-start.11
  220.0 3.1 copy-start.6
  227.6 1.9 copy-start.5
  227.6 2.1 copy-start.12
  284.4 1.7 copy-start.4
  333.7 0.8 copy-start.17
  336.0 1.7 copy-start.3
  385.2 0.8 copy-start.19
  387.5 1.7 copy-start.2
  394.0 48.4 %copy-start.15 = (bf16[320,8,128]{0,2,1:T(8,128)(2,1)S(1)}, bf16[320,8,128]{0,2,1:T(8,128)(2,1)}, u32[]{:S(2)}) copy-start(bf16[320,8,128]{0,2,1:T(8,128)(2,1)} %get-tuple-element.265) | copy-start | bytes 1966084
  442.9 1.7 copy-start.1
  449.6 48.7 %copy-start.14 = (bf16[320,8,128]{0,2,1:T(8,128)(2,1)S(1)}, bf16[320,8,128]{0,2,1:T(8,128)(2,1)}, u32[]{:S(2)}) copy-start(bf16[320,8,128]{0,2,1:T(8,128)(2,1)} %get-tuple-element.267) | copy-start | bytes 1966084
  498.7 1.7 copy-start
  504.5 43.5 %copy-start.18 = (f32[8,64,256]{2,1,0:T(8,128)S(1)}, f32[8,64,256]{2,1,0:T(8,128)}, u32[]{:S(2)}) copy-start(f32[8,64,256]{2,1,0:T(8,128)} %copy-done.17) | copy-start | bytes 1572868
  504.5 43.5 %copy-start.20 = (f32[8,64,256]{2,1,0:T(8,128)S(1)}, f32[8,64,256]{2,1,0:T(8,128)}, u32[]{:S(2)}) copy-start(f32[8,64,256]{2,1,0:T(8,128)} %copy-done.19) | copy-start | bytes 1572868
  504.5 43.5 %copy-start.22 = (f32[129,128]{1,0:T(8,128)S(1)}, f32[129,128]{1,0:T(8,128)}, u32[]{:S(2)}) copy-start(f32[129,128]{1,0:T(8,128)} %fusion.122) | copy-start | bytes 198148
  504.5 43.5 %copy-start.23 = (f32[127,128]{1,0:T(8,128)S(1)}, f32[127,128]{1,0:T(8,128)}, u32[]{:S(2)}) copy-start(f32[127,128]{1,0:T(8,128)} %fusion.135) | copy-start | bytes 195076
where the time goes:
time: 698 us; the launch traced here: 686 us
  other arithmetic  160 us (23%)
  local copies, waits for them, and re-layouts  143 us (20%)
  blocking collectives  134 us (19%)
  loops' own time  94.5 us (14%)
  matrix products  65.1 us (9%)
  waiting for transfers between devices  61.2 us (9%)
  starting transfers between devices  27 us (4%)
    psum x1, blocking collectives, local(): lax.psum(partial_sum, ('grp', 'dev'))  134 us
    another operation x6, loops' own time, local(): spectra_terms = lax.map(offset_terms, offsets)  94.5 us
    reduce_sum x48, other arithmetic, cross_spectra(): jnp.sum(own_real * far_real + own_imag_full * far_imag_full, axis=-2)  67.2 us
    reduce_sum x48, other arithmetic, cross_spectra(): jnp.sum(own_real[..., 1:BLK] * far_imag - own_imag * far_real[..., 1:BLK]...  66.3 us
    ppermute x8, waiting for transfers between devices, shifted(): return lax.ppermute(block, axis, route)  61.2 us
    unnamed x78, local copies, waits for them, and re-layouts  44 us
    dot_general x18, matrix products, table_product(): jnp.dot(records, parts[1], preferred_element_type=jnp.float32)  42.8 us
    dynamic_slice x48, local copies, waits for them, and re-layouts, local(): spectra_terms = lax.map(offset_terms, offsets)  28 us
  transfers between devices with their start and end apart: 8, of which 2 were waited for; matrix products, arithmetic and copies ran while one was open for 6% of the time, Pallas kernels for 0%

commit v1 on v0

--- a/solution.py
+++ b/solution.py
@@ -150,7 +150,7 @@
     divisor = jnp.maximum(pair_count, 1.0)[:, :, None] * math.sqrt(SAMP)
     corr = jnp.transpose(lag_values / divisor, (1, 0, 2))
     partial_sum = jnp.sum(corr, axis=0)
-    stack = lax.psum(partial_sum, ("grp", "dev")) / math.sqrt(
+    stack = jnp.sum(lax.all_gather(partial_sum, ("grp", "dev")), axis=0) / math.sqrt(
         channels * lax.axis_size(("grp", "dev"))
     )
     return (corr, stack)

time: 698 us -> 1170 us (1.68)
  waiting for transfers between devices: 61.2 us -> 649 us
  blocking collectives: 134 us -> 0 us
  between operations: 1.5 us -> 14.9 us
    all_gather x0 -> x1, waiting for transfers between devices: none -> 588 us  [local(): lax.all_gather(partial_sum, ('grp', 'dev'))]
    psum x1 -> x0, blocking collectives: 134 us -> none  [local(): lax.psum(partial_sum, ('grp', 'dev'))]
  transfers between devices with their start and end apart: 8 -> 9, of which waited for: 2 -> 3; matrix products, arithmetic and copies ran while one was open for 6% -> 4% of each run, Pallas kernels for 0% -> 0%
where the time goes in v1:
time: 1170 us; the launch traced here: 1160 us
  waiting for transfers between devices  649 us (55%)
  other arithmetic  162 us (14%)
  local copies, waits for them, and re-layouts  143 us (12%)
  loops' own time  94.5 us (8%)
  matrix products  65.8 us (6%)
  starting transfers between devices  27.1 us (2%)
  between operations  14.9 us (1%)
    all_gather x1, waiting for transfers between devices, local(): lax.all_gather(partial_sum, ('grp', 'dev'))  588 us
    another operation x6, loops' own time, local(): spectra_terms = lax.map(offset_terms, offsets)  94.5 us
    reduce_sum x48, other arithmetic, cross_spectra(): jnp.sum(own_real * far_real + own_imag_full * far_imag_full, axis=-2)  67.2 us
    reduce_sum x48, other arithmetic, cross_spectra(): jnp.sum(own_real[..., 1:BLK] * far_imag - own_imag * far_real[..., 1:BLK]...  66.3 us
    ppermute x8, waiting for transfers between devices, shifted(): return lax.ppermute(block, axis, route)  61.2 us
    unnamed x78, local copies, waits for them, and re-layouts  44 us
    dot_general x18, matrix products, table_product(): jnp.dot(records, parts[1], preferred_element_type=jnp.float32)  42.8 us
    dynamic_slice x48, local copies, waits for them, and re-layouts, local(): spectra_terms = lax.map(offset_terms, offsets)  28 us
  transfers between devices with their start and end apart: 9, of which 3 were waited for; matrix products, arithmetic and copies ran while one was open for 4% of the time, Pallas kernels for 0%

profile of v1, /device:TPU:1, one launch (start us, length us, event | category | flops | bytes accessed | tf_op | source)
XLA Modules:
  0.0 1155.7 jit_solution(10586143398765044812)
XLA Ops:
  8.0 7.9 collective-permute-start
  17.8 5.0 collective-permute-start.3
  24.5 3.2 tile.4
  27.8 10.9 tile.10
  60.6 9.1 collective-permute-start.7
  74.8 21.4 %collective-permute-done.5 = bf16[64,6,1024]{2,0,1:T(8,128)(2,1)} collective-permute-done((bf16[64,6,1024]{2,0,1:T(8,128)(2,1)}, bf16[64,6,1024]{2,0,1:T(8,128)(2,1)}, u32[]{:S(2)}, u32[]{:S(2)}) %collective-permute-start.5) | collective-permute-done | bytes 786464 | tf_op jit(solution)/shard_map/ppermute | solution.py:17
  98.3 39.8 %collective-permute-done.6 = bf16[64,6,1024]{2,0,1:T(8,128)(2,1)} collective-permute-done((bf16[64,6,1024]{2,0,1:T(8,128)(2,1)}, bf16[64,6,1024]{2,0,1:T(8,128)(2,1)}, u32[]{:S(2)}, u32[]{:S(2)}) %collective-permute-start.6) | collective-permute-done | bytes 786464 | tf_op jit(solution)/shard_map/ppermute | solution.py:17
  140.3 2.2 fusion.105
  142.5 2.4 concatenate.117
  147.0 2.8 fusion.189
  149.8 2.4 copy.80
  152.2 3.1 fusion.161
  157.4 2.4 concatenate.120
  161.9 2.8 fusion.190
  164.7 2.4 copy.82
  167.1 3.2 fusion.198
  172.3 2.4 concatenate.122
  176.9 2.8 fusion.191
  179.7 2.4 copy.84
  182.1 3.1 fusion.199
  187.2 2.4 concatenate.124
  191.7 2.8 fusion.192
  194.5 2.4 copy.86
  196.9 3.2 fusion.200
  202.1 2.4 concatenate.126
  206.6 2.7 fusion.193
  209.4 2.4 copy.88
  211.8 3.1 fusion.201
  217.0 2.4 concatenate.128
  219.4 2.4 copy.75
  221.8 2.8 fusion.194
  224.5 2.4 copy.90
  226.9 3.2 fusion.202
  232.1 2.4 copy.81
  236.6 3.9 add_add_fusion.5
  241.3 48.5 %while.60 = (s32[]{:T(128)}, f32[8,64,256]{2,1,0:T(8,128)}, f32[64,8,256]{2,1,0:T(8,128)S(1)}, s32[8]{0:T(128)S(1)}, f32[320,8,256]{2,1,0:T(8,128)}, /*index=5*/...) while((s32[]{:T(128)}, f32[8,64,256]{2,1,0:T(8,128)}, f32[64,8,256]{2,1,0:T(8,128)S(1)}, ...), condition=%wide.region_3.4_spmd, body=%wide.region_0.3_spmd.sunk | while | flops 788487 | bytes 2810567 | solution.py:147
  293.1 4.0 add_add_fusion.4
  297.1 43.5 %while.61 = (s32[]{:T(128)}, f32[8,64,256]{2,1,0:T(8,128)S(1)}, f32[64,8,256]{2,1,0:T(8,128)S(1)}, s32[8]{0:T(128)S(1)}, f32[320,8,256]{2,1,0:T(8,128)}, /*index...) while((s32[]{:T(128)}, f32[8,64,256]{2,1,0:T(8,128)S(1)}, ...), condition=%wide.region_7.8_spmd, body=%wide.region_4.7_spmd.sunk | while | flops 788487 | bytes 2842827 | solution.py:147
  344.7 3.9 add_add_fusion.3
  348.6 43.5 %while.62 = (s32[]{:T(128)}, f32[8,64,256]{2,1,0:T(8,128)S(1)}, f32[64,8,256]{2,1,0:T(8,128)S(1)}, s32[8]{0:T(128)S(1)}, f32[320,8,256]{2,1,0:T(8,128)}, /*index...) while((s32[]{:T(128)}, f32[8,64,256]{2,1,0:T(8,128)S(1)}, ...), condition=%wide.region_11.12_spmd, body=%wide.region_8.11_spmd.sunk | while | flops 788487 | bytes 2842827 | solution.py:147
  396.2 3.9 add_add_fusion.2
  401.0 48.4 %while.63 = (s32[]{:T(128)}, f32[8,64,256]{2,1,0:T(8,128)}, f32[64,8,256]{2,1,0:T(8,128)S(1)}, s32[8]{0:T(128)S(1)}, f32[320,8,256]{2,1,0:T(8,128)}, /*index=5*/...) while((s32[]{:T(128)}, f32[8,64,256]{2,1,0:T(8,128)}, f32[64,8,256]{2,1,0:T(8,128)S(1)}, ...), condition=%wide.region_15.16_spmd, body=%wide.region_12.15_spmd.sunk | while | flops 788487 | bytes 2810567 | solution.py:147
  451.6 4.0 add_add_fusion.1
  456.5 48.7 %while.64 = (s32[]{:T(128)}, f32[8,64,256]{2,1,0:T(8,128)}, f32[64,8,256]{2,1,0:T(8,128)S(1)}, s32[8]{0:T(128)S(1)}, f32[320,8,256]{2,1,0:T(8,128)}, /*index=5*/...) while((s32[]{:T(128)}, f32[8,64,256]{2,1,0:T(8,128)}, f32[64,8,256]{2,1,0:T(8,128)S(1)}, ...), condition=%wide.region_19.20_spmd, body=%wide.region_16.19_spmd.sunk | while | flops 788487 | bytes 2810567 | solution.py:147
  507.4 4.0 add_add_fusion
  511.5 43.5 %while.65 = (s32[]{:T(128)}, f32[8,64,256]{2,1,0:T(8,128)S(1)}, f32[64,8,256]{2,1,0:T(8,128)S(1)}, s32[8]{0:T(128)S(1)}, f32[320,8,256]{2,1,0:T(8,128)}, /*index...) while((s32[]{:T(128)}, f32[8,64,256]{2,1,0:T(8,128)S(1)}, ...), condition=%wide.region_23.24_spmd, body=%wide.region_20.23_spmd.sunk | while | flops 788487 | bytes 2842827 | solution.py:147
  555.0 2.9 fusion.196
  558.8 587.7 %all-gather.3.cloned.1.call-done = f32[2048,128]{1,0:T(8,128)} async-done(((f32[8,128]{1,0:T(8,128)}), f32[2048,128]{1,0:T(8,128)}) %all-gather.3.cloned.1.call-update) | async-done | bytes 1048592 | tf_op jit(solution)/shard_map/all_gather | solution.py:153
  (397 shorter events, 263.7 us)
Async XLA Ops:
  7.2 17.1 %copy-start.24 = (bf16[64,64]{1,0:T(8,128)(2,1)S(1)}, bf16[64,64]{1,0:T(8,128)(2,1)}, u32[]{:S(2)}) copy-start(bf16[64,64]{1,0:T(8,128)(2,1)} %param.17) | copy-start | bytes 24580
  7.2 1139.3 %all-gather.3.cloned.1.call-start = ((), (), s32[]{:S(2)}) async-start(), calls=%async_computation | async-start | bytes 1052672 | tf_op jit(solution)/shard_map/all_gather | solution.py:153
  8.0 51.0 %collective-permute-start = (bf16[64,6]{0,1:T(8,128)(2,1)S(1)}, bf16[64,6]{0,1:T(8,128)(2,1)S(1)}, u32[]{:S(2)}, u32[]{:S(2)}) collective-permute-start(bf16[64,6]{0,1:T(8,128)(2,1)S(1)} %get-tuple-element.317), channel_id=1, source_target_pairs={{1,0},{2,1},{3,2},{4,3},{5,4},{6,5},{7,6},{8,7},{9,8},{10,9},{11,1... | collective-permute-start | bytes 2312 | tf_op jit(solution)/shard_map/ppermute | solution.py:17
  15.9 43.8 %collective-permute-start.1 = (bf16[64,6]{0,1:T(8,128)(2,1)S(1)}, bf16[64,6]{0,1:T(8,128)(2,1)S(1)}, u32[]{:S(2)}, u32[]{:S(2)}) collective-permute-start(bf16[64,6]{0,1:T(8,128)(2,1)S(1)} %get-tuple-element.317), channel_id=1, source_target_pairs={{2,0},{3,1},{4,2},{5,3},{6,4},{7,5},{8,6},{9,7},{10,8},{11,9},{12,... | collective-permute-start | bytes 2312 | tf_op jit(solution)/shard_map/ppermute | solution.py:17
  17.3 43.2 %collective-permute-start.2 = (bf16[64,6]{0,1:T(8,128)(2,1)S(1)}, bf16[64,6]{0,1:T(8,128)(2,1)S(1)}, u32[]{:S(2)}, u32[]{:S(2)}) collective-permute-start(bf16[64,6]{0,1:T(8,128)(2,1)S(1)} %get-tuple-element.317), channel_id=1, source_target_pairs={{3,0},{4,1},{5,2},{6,3},{7,4},{8,5},{9,6},{10,7},{11,8},{12,9},{13... | collective-permute-start | bytes 2312 | tf_op jit(solution)/shard_map/ppermute | solution.py:17
  17.8 51.9 %collective-permute-start.3 = (bf16[64,6]{0,1:T(8,128)(2,1)S(1)}, bf16[64,6]{0,1:T(8,128)(2,1)S(1)}, u32[]{:S(2)}, u32[]{:S(2)}) collective-permute-start(bf16[64,6]{0,1:T(8,128)(2,1)S(1)} %get-tuple-element.317), channel_id=1, source_target_pairs={{4,0},{5,1},{6,2},{7,3},{8,4},{9,5},{10,6},{11,7},{12,8},{13,9},{1... | collective-permute-start | bytes 2312 | tf_op jit(solution)/shard_map/ppermute | solution.py:17
  38.6 2.2 slice-start
  44.9 27.8 %collective-permute-start.4 = (bf16[64,6,1024]{2,0,1:T(8,128)(2,1)}, bf16[64,6,1024]{2,0,1:T(8,128)(2,1)}, u32[]{:S(2)}, u32[]{:S(2)}) collective-permute-start(bf16[64,6,1024]{2,0,1:T(8,128)(2,1)} %convert_element_type.64), channel_id=1, source_target_pairs={{1,0},{2,1},{3,2},{4,3},{5,4},{6,5},{7,6},{8,7},{9,8},{10,9},{11,1... | collective-permute-start | bytes 2359304 | tf_op jit(solution)/shard_map/ppermute | solution.py:17
  49.5 4.6 copy-start.16
  51.4 2.0 copy-start.21
  55.0 1.2 copy-start.25
  59.0 37.2 %collective-permute-start.5 = (bf16[64,6,1024]{2,0,1:T(8,128)(2,1)}, bf16[64,6,1024]{2,0,1:T(8,128)(2,1)}, u32[]{:S(2)}, u32[]{:S(2)}) collective-permute-start(bf16[64,6,1024]{2,0,1:T(8,128)(2,1)} %convert_element_type.64), channel_id=1, source_target_pairs={{2,0},{3,1},{4,2},{5,3},{6,4},{7,5},{8,6},{9,7},{10,8},{11,9},{12,... | collective-permute-start | bytes 2359304 | tf_op jit(solution)/shard_map/ppermute | solution.py:17
  59.6 78.5 %collective-permute-start.6 = (bf16[64,6,1024]{2,0,1:T(8,128)(2,1)}, bf16[64,6,1024]{2,0,1:T(8,128)(2,1)}, u32[]{:S(2)}, u32[]{:S(2)}) collective-permute-start(bf16[64,6,1024]{2,0,1:T(8,128)(2,1)} %convert_element_type.64), channel_id=1, source_target_pairs={{3,0},{4,1},{5,2},{6,3},{7,4},{8,5},{9,6},{10,7},{11,8},{12,9},{13... | collective-permute-start | bytes 2359304 | tf_op jit(solution)/shard_map/ppermute | solution.py:17
  60.6 79.7 %collective-permute-start.7 = (bf16[64,6,1024]{2,0,1:T(8,128)(2,1)}, bf16[64,6,1024]{2,0,1:T(8,128)(2,1)}, u32[]{:S(2)}, u32[]{:S(2)}) collective-permute-start(bf16[64,6,1024]{2,0,1:T(8,128)(2,1)} %convert_element_type.64), channel_id=1, source_target_pairs={{4,0},{5,1},{6,2},{7,3},{8,4},{9,5},{10,6},{11,7},{12,8},{13,9},{1... | collective-permute-start | bytes 2359304 | tf_op jit(solution)/shard_map/ppermute | solution.py:17
  149.8 5.5 copy-start.13
  152.2 3.1 copy-start.7
  167.1 3.2 copy-start.8
  182.1 3.1 copy-start.9
  196.9 3.2 copy-start.10
  211.8 3.1 copy-start.11
  226.9 3.2 copy-start.6
  234.5 1.9 copy-start.5
  234.5 2.1 copy-start.12
  291.4 1.7 copy-start.4
  340.6 0.8 copy-start.17
  343.0 1.7 copy-start.3
  392.1 0.8 copy-start.19
  394.5 1.7 copy-start.2
  401.0 48.4 %copy-start.15 = (bf16[320,8,128]{0,2,1:T(8,128)(2,1)S(1)}, bf16[320,8,128]{0,2,1:T(8,128)(2,1)}, u32[]{:S(2)}) copy-start(bf16[320,8,128]{0,2,1:T(8,128)(2,1)} %get-tuple-element.267) | copy-start | bytes 1966084
  449.9 1.7 copy-start.1
  456.5 48.7 %copy-start.14 = (bf16[320,8,128]{0,2,1:T(8,128)(2,1)S(1)}, bf16[320,8,128]{0,2,1:T(8,128)(2,1)}, u32[]{:S(2)}) copy-start(bf16[320,8,128]{0,2,1:T(8,128)(2,1)} %get-tuple-element.269) | copy-start | bytes 1966084
  505.7 1.7 copy-start
  511.5 43.5 %copy-start.18 = (f32[8,64,256]{2,1,0:T(8,128)S(1)}, f32[8,64,256]{2,1,0:T(8,128)}, u32[]{:S(2)}) copy-start(f32[8,64,256]{2,1,0:T(8,128)} %copy-done.17) | copy-start | bytes 1572868
  511.5 43.5 %copy-start.20 = (f32[8,64,256]{2,1,0:T(8,128)S(1)}, f32[8,64,256]{2,1,0:T(8,128)}, u32[]{:S(2)}) copy-start(f32[8,64,256]{2,1,0:T(8,128)} %copy-done.19) | copy-start | bytes 1572868
  511.5 43.5 %copy-start.22 = (f32[129,128]{1,0:T(8,128)S(1)}, f32[129,128]{1,0:T(8,128)}, u32[]{:S(2)}) copy-start(f32[129,128]{1,0:T(8,128)} %fusion.122) | copy-start | bytes 198148
  511.5 43.5 %copy-start.23 = (f32[127,128]{1,0:T(8,128)S(1)}, f32[127,128]{1,0:T(8,128)}, u32[]{:S(2)}) copy-start(f32[127,128]{1,0:T(8,128)} %fusion.135) | copy-start | bytes 195076
Sparse Core Ops, SparseCore 0:
  558.0 588.4 all-gather.2
